TPU v7x, 32 devices: a whole 2x2x4 slice. The times are simulated.
32 devices in a mesh: grp: 2 (over x), row: 16 (over z, y, core).
Axes of the slice: x: 2, y: 2, z: 4, core: 2. Of those that a mesh axis runs over, the one named last changes fastest.
Arguments:
- sources: bfloat16 [32, 8, 8, 1024], P(('grp', 'row')), parts along dimension 0, may hold values from -6 to 6
- far_left: bfloat16 [64, 15, 48, 1024], P(('grp', 'row')), parts along dimension 0, may hold values from -0.1875 to 0.1875
- far_right: bfloat16 [64, 15, 48, 1024], P(('grp', 'row')), parts along dimension 0, may hold values from -0.078125 to 0.078125
- ranks: int32 [64, 15], P(('grp', 'row')), parts along dimension 0, may hold values from 16 to 48
- near_blocks: bfloat16 [6, 1024, 1024], P('grp'), parts along dimension 0, may hold values from -0.1875 to 0.1875
- near_offsets: int32 [6, 2], P('grp'), parts along dimension 0, may hold values from -1 to 1, as said below
Outputs:
- fields: float32 [32, 8, 8, 1024], P(('grp', 'row')), parts along dimension 0
There are 2 independent parts, one for each index of `grp`. A program takes and returns all parts, laid end to end along the dimension named above; each array names one. Nothing has to cross between parts.
Inputs may be any that keep to these rules, and one draw needn't show every extreme that they name: `near_offsets`: the rows are 3 distinct offsets (a, b); row 0 is the self offset (0, 0).
All inputs are finite; a program needn't handle non-finite values.
Results may differ from a plain program's by a relative error of at most 0.0014.
Values may be sent and summed in bfloat16 or wider, within the bound.
A program may use at most 64 MiB of HBM per device.

v0:
```python
import jax
import jax.numpy as jnp
from jax import lax
from jax.sharding import PartitionSpec as P

RANK = 48
ECOL = 8
SLOTS = 15


def from_behind(value, axis, by):
    count = lax.axis_size(axis)
    return lax.ppermute(value, axis, [(i, (i + by) % count) for i in range(count)])


def padded_2(block, sides, width):
    for axis, dim in sides:
        count = lax.axis_size(axis)
        forward = [(i, i + 1) for i in range(count - 1)]
        backward = [(target, source) for source, target in forward]
        low = lax.ppermute(
            lax.slice_in_dim(block, block.shape[dim] - width, None, axis=dim), axis, forward
        )
        high = lax.ppermute(lax.slice_in_dim(block, 0, width, axis=dim), axis, backward)
        block = jnp.concatenate([low, block, high], axis=dim)
    return block


def slot_mask(rank_row, row_offset, near_offsets):
    col_offset = jnp.arange(SLOTS, dtype=jnp.int32) - (ECOL - 1)
    hit = jnp.any(
        (near_offsets[:, 0][:, None] == row_offset)
        & (near_offsets[:, 1][:, None] == col_offset[None, :]),
        axis=0,
    )
    live = jnp.arange(RANK, dtype=jnp.int32)[None, :] < rank_row[:, None]
    return (live & jnp.logical_not(hit)[:, None]).astype(jnp.float32)


def spread(coeffs):
    padded = jnp.pad(coeffs, ((ECOL, ECOL), (0, 0), (0, 0), (0, 0)))
    columns = [padded[2 * ECOL - 1 - k : 3 * ECOL - 1 - k, k, :, :] for k in range(SLOTS)]
    return jnp.stack(columns, axis=1)


def far_term(source_row, left, right, keep):
    coeffs = jnp.einsum("sbn,krn->skbr", source_row, left, preferred_element_type=jnp.float32)
    coeffs = (coeffs * keep[None, :, None, :]).astype(jnp.bfloat16)
    return jnp.einsum("jkbr,krn->jbn", spread(coeffs), right, preferred_element_type=jnp.float32)


def local(sources, far_left, far_right, ranks, near_blocks, near_offsets):
    cycle_size = lax.axis_size("row")
    place = lax.axis_index("row")
    keep_all = jnp.stack(
        [slot_mask(ranks[w], place - cycle_size * w, near_offsets) for w in range(2)], axis=0
    )
    ecol, beams, width = (sources.shape[1], sources.shape[2], sources.shape[3])

    def source_term(source_row, source_index):
        wrap_bit = (source_index + place >= cycle_size).astype(jnp.int32)
        left = lax.dynamic_index_in_dim(far_left, wrap_bit, 0, keepdims=False)
        right = lax.dynamic_index_in_dim(far_right, wrap_bit, 0, keepdims=False)
        keep = lax.dynamic_index_in_dim(keep_all, wrap_bit, 0, keepdims=False)
        return far_term(source_row, left, right, keep)

    gathered = lax.all_gather(sources, "row", axis=0, tiled=True)

    def step(source_index, accums):
        down_acc, up_acc = accums
        source_row = lax.dynamic_index_in_dim(gathered, source_index, 0, keepdims=False)
        down_acc = down_acc + source_term(source_row, source_index)
        down_acc = from_behind(down_acc, "row", -1)
        return (down_acc, up_acc)

    start = (jnp.zeros((ecol, beams, width), jnp.float32), jnp.zeros((1,), jnp.float32))
    far, unused_up = lax.fori_loop(0, cycle_size, step, start)
    beside = padded_2(sources, (("row", 0),), 1)
    beside = jnp.pad(beside, ((0, 0), (1, 1), (0, 0), (0, 0)))
    near = jnp.zeros((ecol * beams, width), jnp.float32)
    for index in range(near_blocks.shape[0]):
        row_offset = near_offsets[index, 0]
        col_offset = near_offsets[index, 1]
        anchor = (1 - row_offset, 1 - col_offset, jnp.int32(0), jnp.int32(0))
        shifted = lax.dynamic_slice(beside, anchor, (1, ecol, beams, width))
        near = near + jnp.dot(
            shifted.reshape(-1, width), near_blocks[index], preferred_element_type=jnp.float32
        )
    return (near.reshape(ecol, beams, width) + far).reshape(1, ecol, beams, width)


def solution(mesh):
    placed = (
        P(("grp", "row"), None, None, None),
        P(("grp", "row"), None, None, None),
        P(("grp", "row"), None, None, None),
        P(("grp", "row"), None),
        P("grp", None, None),
        P("grp", None),
    )
    return jax.shard_map(
        local,
        mesh=mesh,
        in_specs=placed,
        out_specs=P(("grp", "row"), None, None, None),
        check_vma=False,
    )
```

profile of v0, /device:TPU:0, one launch (start us, length us, event | category | flops | bytes accessed | tf_op | source)
XLA Modules:
  0.0 249.0 jit_solution(835424933795626141)
XLA Ops:
  7.3 2.4 collective-permute-start.1
  23.3 3.0 %fusion.25 = f32[64,1024]{1,0:T(8,128)} fusion(bf16[3,1024,1024]{2,1,0:T(8,128)(2,1)} %param.12, bf16[3,10,8,1024]{3,2,1,0:T(8,128)(2,1)S(1)} %fusion.54, s32[]{:T(128)S(6)} %select_n.45, s32[]{:T(128)S(6)} %select_n.46), kind=kOutput, calls=%fused_computation.45 | convolution fusion | flops 134217728 | bytes 2490376 | tf_op jit(solution)/shard_map/dot_general | solution.py:86
  26.2 2.8 %fusion.27 = f32[64,1024]{1,0:T(8,128)} fusion(bf16[3,1024,1024]{2,1,0:T(8,128)(2,1)} %param.12, bf16[3,10,8,1024]{3,2,1,0:T(8,128)(2,1)S(1)} %fusion.54, s32[]{:T(128)S(6)} %select_n.43, s32[]{:T(128)S(6)} %select_n.44), kind=kOutput, calls=%fused_computation.47 | convolution fusion | flops 134217728 | bytes 2490376 | tf_op jit(solution)/shard_map/dot_general | solution.py:86
  29.0 24.7 %all-gather.2.cloned.1.call-done = bf16[16,8,8,1024]{3,2,1,0:T(8,128)(2,1)} async-done(((bf16[1,8,8,1024]{3,2,1,0:T(8,128)(2,1)}), bf16[16,8,8,1024]{3,2,1,0:T(8,128)(2,1)}) %all-gather.2.cloned.1.call-update) | async-done | bytes 2097168 | tf_op jit(solution)/shard_map/all_gather | solution.py:67
  53.7 185.6 %while.15 = (s32[]{:T(128)}, f32[8,8,1024]{2,1,0:T(8,128)S(1)}, s32[]{:T(128)}, bf16[2,15,48,1024]{3,2,1,0:T(8,128)(2,1)}, bf16[16,8,8,1024]{3,2,1,0:T(8,128)(2,...) while((s32[]{:T(128)}, f32[8,8,1024]{2,1,0:T(8,128)S(1)}, ...), condition=%wide.region_3.4_spmd, body=%wide.region_2.3_spmd.sunk | while | flops 188901376 | bytes 8549533 | solution.py:77
  53.7 2.3 fusion.80
  59.0 3.9 %collective-permute-done = f32[8,8,1024]{2,1,0:T(8,128)S(1)} collective-permute-done((f32[8,8,1024]{2,1,0:T(8,128)S(1)}, f32[8,8,1024]{2,1,0:T(8,128)S(1)}, u32[]{:S(2)}, u32[]{:S(2)}) %collective-permute-start) | collective-permute-done | bytes 262176 | tf_op jit(solution)/shard_map/while/body/eval_jaxpr/ppermute | solution.py:13
  66.1 4.7 %collective-permute-start = (f32[8,8,1024]{2,1,0:T(8,128)S(1)}, f32[8,8,1024]{2,1,0:T(8,128)S(1)}, u32[]{:S(2)}, u32[]{:S(2)}) collective-permute-start(f32[8,8,1024]{2,1,0:T(8,128)S(1)} %fusion.81), channel_id=1, source_target_pairs={{0,15},{1,0},{2,1},{3,2},{4,3},{5,4},{6,5},{7,6},{8,7},{9,8},{10,9... | collective-permute-start | bytes 786440 | tf_op jit(solution)/shard_map/while/body/eval_jaxpr/ppermute | solution.py:13
  70.7 3.9 %collective-permute-done = f32[8,8,1024]{2,1,0:T(8,128)S(1)} collective-permute-done((f32[8,8,1024]{2,1,0:T(8,128)S(1)}, f32[8,8,1024]{2,1,0:T(8,128)S(1)}, u32[]{:S(2)}, u32[]{:S(2)}) %collective-permute-start) | collective-permute-done | bytes 262176 | tf_op jit(solution)/shard_map/while/body/eval_jaxpr/ppermute | solution.py:13
  74.6 2.3 fusion.80
  77.8 4.7 %collective-permute-start = (f32[8,8,1024]{2,1,0:T(8,128)S(1)}, f32[8,8,1024]{2,1,0:T(8,128)S(1)}, u32[]{:S(2)}, u32[]{:S(2)}) collective-permute-start(f32[8,8,1024]{2,1,0:T(8,128)S(1)} %fusion.81), channel_id=1, source_target_pairs={{0,15},{1,0},{2,1},{3,2},{4,3},{5,4},{6,5},{7,6},{8,7},{9,8},{10,9... | collective-permute-start | bytes 786440 | tf_op jit(solution)/shard_map/while/body/eval_jaxpr/ppermute | solution.py:13
  82.5 3.9 %collective-permute-done = f32[8,8,1024]{2,1,0:T(8,128)S(1)} collective-permute-done((f32[8,8,1024]{2,1,0:T(8,128)S(1)}, f32[8,8,1024]{2,1,0:T(8,128)S(1)}, u32[]{:S(2)}, u32[]{:S(2)}) %collective-permute-start) | collective-permute-done | bytes 262176 | tf_op jit(solution)/shard_map/while/body/eval_jaxpr/ppermute | solution.py:13
  86.4 2.3 fusion.80
  89.6 4.7 %collective-permute-start = (f32[8,8,1024]{2,1,0:T(8,128)S(1)}, f32[8,8,1024]{2,1,0:T(8,128)S(1)}, u32[]{:S(2)}, u32[]{:S(2)}) collective-permute-start(f32[8,8,1024]{2,1,0:T(8,128)S(1)} %fusion.81), channel_id=1, source_target_pairs={{0,15},{1,0},{2,1},{3,2},{4,3},{5,4},{6,5},{7,6},{8,7},{9,8},{10,9... | collective-permute-start | bytes 786440 | tf_op jit(solution)/shard_map/while/body/eval_jaxpr/ppermute | solution.py:13
  94.2 3.9 %collective-permute-done = f32[8,8,1024]{2,1,0:T(8,128)S(1)} collective-permute-done((f32[8,8,1024]{2,1,0:T(8,128)S(1)}, f32[8,8,1024]{2,1,0:T(8,128)S(1)}, u32[]{:S(2)}, u32[]{:S(2)}) %collective-permute-start) | collective-permute-done | bytes 262176 | tf_op jit(solution)/shard_map/while/body/eval_jaxpr/ppermute | solution.py:13
  98.1 2.3 fusion.80
  101.4 4.7 %collective-permute-start = (f32[8,8,1024]{2,1,0:T(8,128)S(1)}, f32[8,8,1024]{2,1,0:T(8,128)S(1)}, u32[]{:S(2)}, u32[]{:S(2)}) collective-permute-start(f32[8,8,1024]{2,1,0:T(8,128)S(1)} %fusion.81), channel_id=1, source_target_pairs={{0,15},{1,0},{2,1},{3,2},{4,3},{5,4},{6,5},{7,6},{8,7},{9,8},{10,9... | collective-permute-start | bytes 786440 | tf_op jit(solution)/shard_map/while/body/eval_jaxpr/ppermute | solution.py:13
  106.0 3.9 %collective-permute-done = f32[8,8,1024]{2,1,0:T(8,128)S(1)} collective-permute-done((f32[8,8,1024]{2,1,0:T(8,128)S(1)}, f32[8,8,1024]{2,1,0:T(8,128)S(1)}, u32[]{:S(2)}, u32[]{:S(2)}) %collective-permute-start) | collective-permute-done | bytes 262176 | tf_op jit(solution)/shard_map/while/body/eval_jaxpr/ppermute | solution.py:13
  109.9 2.3 fusion.80
  113.1 4.7 %collective-permute-start = (f32[8,8,1024]{2,1,0:T(8,128)S(1)}, f32[8,8,1024]{2,1,0:T(8,128)S(1)}, u32[]{:S(2)}, u32[]{:S(2)}) collective-permute-start(f32[8,8,1024]{2,1,0:T(8,128)S(1)} %fusion.81), channel_id=1, source_target_pairs={{0,15},{1,0},{2,1},{3,2},{4,3},{5,4},{6,5},{7,6},{8,7},{9,8},{10,9... | collective-permute-start | bytes 786440 | tf_op jit(solution)/shard_map/while/body/eval_jaxpr/ppermute | solution.py:13
  117.8 3.9 %collective-permute-done = f32[8,8,1024]{2,1,0:T(8,128)S(1)} collective-permute-done((f32[8,8,1024]{2,1,0:T(8,128)S(1)}, f32[8,8,1024]{2,1,0:T(8,128)S(1)}, u32[]{:S(2)}, u32[]{:S(2)}) %collective-permute-start) | collective-permute-done | bytes 262176 | tf_op jit(solution)/shard_map/while/body/eval_jaxpr/ppermute | solution.py:13
  121.7 2.3 fusion.80
  124.9 4.7 %collective-permute-start = (f32[8,8,1024]{2,1,0:T(8,128)S(1)}, f32[8,8,1024]{2,1,0:T(8,128)S(1)}, u32[]{:S(2)}, u32[]{:S(2)}) collective-permute-start(f32[8,8,1024]{2,1,0:T(8,128)S(1)} %fusion.81), channel_id=1, source_target_pairs={{0,15},{1,0},{2,1},{3,2},{4,3},{5,4},{6,5},{7,6},{8,7},{9,8},{10,9... | collective-permute-start | bytes 786440 | tf_op jit(solution)/shard_map/while/body/eval_jaxpr/ppermute | solution.py:13
  129.5 3.9 %collective-permute-done = f32[8,8,1024]{2,1,0:T(8,128)S(1)} collective-permute-done((f32[8,8,1024]{2,1,0:T(8,128)S(1)}, f32[8,8,1024]{2,1,0:T(8,128)S(1)}, u32[]{:S(2)}, u32[]{:S(2)}) %collective-permute-start) | collective-permute-done | bytes 262176 | tf_op jit(solution)/shard_map/while/body/eval_jaxpr/ppermute | solution.py:13
  133.4 2.3 fusion.80
  136.6 4.7 %collective-permute-start = (f32[8,8,1024]{2,1,0:T(8,128)S(1)}, f32[8,8,1024]{2,1,0:T(8,128)S(1)}, u32[]{:S(2)}, u32[]{:S(2)}) collective-permute-start(f32[8,8,1024]{2,1,0:T(8,128)S(1)} %fusion.81), channel_id=1, source_target_pairs={{0,15},{1,0},{2,1},{3,2},{4,3},{5,4},{6,5},{7,6},{8,7},{9,8},{10,9... | collective-permute-start | bytes 786440 | tf_op jit(solution)/shard_map/while/body/eval_jaxpr/ppermute | solution.py:13
  141.3 3.9 %collective-permute-done = f32[8,8,1024]{2,1,0:T(8,128)S(1)} collective-permute-done((f32[8,8,1024]{2,1,0:T(8,128)S(1)}, f32[8,8,1024]{2,1,0:T(8,128)S(1)}, u32[]{:S(2)}, u32[]{:S(2)}) %collective-permute-start) | collective-permute-done | bytes 262176 | tf_op jit(solution)/shard_map/while/body/eval_jaxpr/ppermute | solution.py:13
  145.2 2.3 fusion.80
  148.4 4.7 %collective-permute-start = (f32[8,8,1024]{2,1,0:T(8,128)S(1)}, f32[8,8,1024]{2,1,0:T(8,128)S(1)}, u32[]{:S(2)}, u32[]{:S(2)}) collective-permute-start(f32[8,8,1024]{2,1,0:T(8,128)S(1)} %fusion.81), channel_id=1, source_target_pairs={{0,15},{1,0},{2,1},{3,2},{4,3},{5,4},{6,5},{7,6},{8,7},{9,8},{10,9... | collective-permute-start | bytes 786440 | tf_op jit(solution)/shard_map/while/body/eval_jaxpr/ppermute | solution.py:13
  153.1 3.9 %collective-permute-done = f32[8,8,1024]{2,1,0:T(8,128)S(1)} collective-permute-done((f32[8,8,1024]{2,1,0:T(8,128)S(1)}, f32[8,8,1024]{2,1,0:T(8,128)S(1)}, u32[]{:S(2)}, u32[]{:S(2)}) %collective-permute-start) | collective-permute-done | bytes 262176 | tf_op jit(solution)/shard_map/while/body/eval_jaxpr/ppermute | solution.py:13
  157.0 2.3 fusion.80
  160.2 4.7 %collective-permute-start = (f32[8,8,1024]{2,1,0:T(8,128)S(1)}, f32[8,8,1024]{2,1,0:T(8,128)S(1)}, u32[]{:S(2)}, u32[]{:S(2)}) collective-permute-start(f32[8,8,1024]{2,1,0:T(8,128)S(1)} %fusion.81), channel_id=1, source_target_pairs={{0,15},{1,0},{2,1},{3,2},{4,3},{5,4},{6,5},{7,6},{8,7},{9,8},{10,9... | collective-permute-start | bytes 786440 | tf_op jit(solution)/shard_map/while/body/eval_jaxpr/ppermute | solution.py:13
  164.8 3.9 %collective-permute-done = f32[8,8,1024]{2,1,0:T(8,128)S(1)} collective-permute-done((f32[8,8,1024]{2,1,0:T(8,128)S(1)}, f32[8,8,1024]{2,1,0:T(8,128)S(1)}, u32[]{:S(2)}, u32[]{:S(2)}) %collective-permute-start) | collective-permute-done | bytes 262176 | tf_op jit(solution)/shard_map/while/body/eval_jaxpr/ppermute | solution.py:13
  168.7 2.3 fusion.80
  171.9 4.7 %collective-permute-start = (f32[8,8,1024]{2,1,0:T(8,128)S(1)}, f32[8,8,1024]{2,1,0:T(8,128)S(1)}, u32[]{:S(2)}, u32[]{:S(2)}) collective-permute-start(f32[8,8,1024]{2,1,0:T(8,128)S(1)} %fusion.81), channel_id=1, source_target_pairs={{0,15},{1,0},{2,1},{3,2},{4,3},{5,4},{6,5},{7,6},{8,7},{9,8},{10,9... | collective-permute-start | bytes 786440 | tf_op jit(solution)/shard_map/while/body/eval_jaxpr/ppermute | solution.py:13
  176.6 3.9 %collective-permute-done = f32[8,8,1024]{2,1,0:T(8,128)S(1)} collective-permute-done((f32[8,8,1024]{2,1,0:T(8,128)S(1)}, f32[8,8,1024]{2,1,0:T(8,128)S(1)}, u32[]{:S(2)}, u32[]{:S(2)}) %collective-permute-start) | collective-permute-done | bytes 262176 | tf_op jit(solution)/shard_map/while/body/eval_jaxpr/ppermute | solution.py:13
  180.5 2.3 fusion.80
  183.7 4.7 %collective-permute-start = (f32[8,8,1024]{2,1,0:T(8,128)S(1)}, f32[8,8,1024]{2,1,0:T(8,128)S(1)}, u32[]{:S(2)}, u32[]{:S(2)}) collective-permute-start(f32[8,8,1024]{2,1,0:T(8,128)S(1)} %fusion.81), channel_id=1, source_target_pairs={{0,15},{1,0},{2,1},{3,2},{4,3},{5,4},{6,5},{7,6},{8,7},{9,8},{10,9... | collective-permute-start | bytes 786440 | tf_op jit(solution)/shard_map/while/body/eval_jaxpr/ppermute | solution.py:13
  188.4 3.9 %collective-permute-done = f32[8,8,1024]{2,1,0:T(8,128)S(1)} collective-permute-done((f32[8,8,1024]{2,1,0:T(8,128)S(1)}, f32[8,8,1024]{2,1,0:T(8,128)S(1)}, u32[]{:S(2)}, u32[]{:S(2)}) %collective-permute-start) | collective-permute-done | bytes 262176 | tf_op jit(solution)/shard_map/while/body/eval_jaxpr/ppermute | solution.py:13
  195.5 4.7 %collective-permute-start = (f32[8,8,1024]{2,1,0:T(8,128)S(1)}, f32[8,8,1024]{2,1,0:T(8,128)S(1)}, u32[]{:S(2)}, u32[]{:S(2)}) collective-permute-start(f32[8,8,1024]{2,1,0:T(8,128)S(1)} %fusion.81), channel_id=1, source_target_pairs={{0,15},{1,0},{2,1},{3,2},{4,3},{5,4},{6,5},{7,6},{8,7},{9,8},{10,9... | collective-permute-start | bytes 786440 | tf_op jit(solution)/shard_map/while/body/eval_jaxpr/ppermute | solution.py:13
  200.1 3.9 %collective-permute-done = f32[8,8,1024]{2,1,0:T(8,128)S(1)} collective-permute-done((f32[8,8,1024]{2,1,0:T(8,128)S(1)}, f32[8,8,1024]{2,1,0:T(8,128)S(1)}, u32[]{:S(2)}, u32[]{:S(2)}) %collective-permute-start) | collective-permute-done | bytes 262176 | tf_op jit(solution)/shard_map/while/body/eval_jaxpr/ppermute | solution.py:13
  207.2 4.7 %collective-permute-start = (f32[8,8,1024]{2,1,0:T(8,128)S(1)}, f32[8,8,1024]{2,1,0:T(8,128)S(1)}, u32[]{:S(2)}, u32[]{:S(2)}) collective-permute-start(f32[8,8,1024]{2,1,0:T(8,128)S(1)} %fusion.81), channel_id=1, source_target_pairs={{0,15},{1,0},{2,1},{3,2},{4,3},{5,4},{6,5},{7,6},{8,7},{9,8},{10,9... | collective-permute-start | bytes 786440 | tf_op jit(solution)/shard_map/while/body/eval_jaxpr/ppermute | solution.py:13
  211.9 3.9 %collective-permute-done = f32[8,8,1024]{2,1,0:T(8,128)S(1)} collective-permute-done((f32[8,8,1024]{2,1,0:T(8,128)S(1)}, f32[8,8,1024]{2,1,0:T(8,128)S(1)}, u32[]{:S(2)}, u32[]{:S(2)}) %collective-permute-start) | collective-permute-done | bytes 262176 | tf_op jit(solution)/shard_map/while/body/eval_jaxpr/ppermute | solution.py:13
  219.0 4.7 %collective-permute-start = (f32[8,8,1024]{2,1,0:T(8,128)S(1)}, f32[8,8,1024]{2,1,0:T(8,128)S(1)}, u32[]{:S(2)}, u32[]{:S(2)}) collective-permute-start(f32[8,8,1024]{2,1,0:T(8,128)S(1)} %fusion.81), channel_id=1, source_target_pairs={{0,15},{1,0},{2,1},{3,2},{4,3},{5,4},{6,5},{7,6},{8,7},{9,8},{10,9... | collective-permute-start | bytes 786440 | tf_op jit(solution)/shard_map/while/body/eval_jaxpr/ppermute | solution.py:13
  223.7 3.9 %collective-permute-done = f32[8,8,1024]{2,1,0:T(8,128)S(1)} collective-permute-done((f32[8,8,1024]{2,1,0:T(8,128)S(1)}, f32[8,8,1024]{2,1,0:T(8,128)S(1)}, u32[]{:S(2)}, u32[]{:S(2)}) %collective-permute-start) | collective-permute-done | bytes 262176 | tf_op jit(solution)/shard_map/while/body/eval_jaxpr/ppermute | solution.py:13
  230.8 4.7 %collective-permute-start = (f32[8,8,1024]{2,1,0:T(8,128)S(1)}, f32[8,8,1024]{2,1,0:T(8,128)S(1)}, u32[]{:S(2)}, u32[]{:S(2)}) collective-permute-start(f32[8,8,1024]{2,1,0:T(8,128)S(1)} %fusion.81), channel_id=1, source_target_pairs={{0,15},{1,0},{2,1},{3,2},{4,3},{5,4},{6,5},{7,6},{8,7},{9,8},{10,9... | collective-permute-start | bytes 786440 | tf_op jit(solution)/shard_map/while/body/eval_jaxpr/ppermute | solution.py:13
  235.4 3.9 %collective-permute-done = f32[8,8,1024]{2,1,0:T(8,128)S(1)} collective-permute-done((f32[8,8,1024]{2,1,0:T(8,128)S(1)}, f32[8,8,1024]{2,1,0:T(8,128)S(1)}, u32[]{:S(2)}, u32[]{:S(2)}) %collective-permute-start) | collective-permute-done | bytes 262176 | tf_op jit(solution)/shard_map/while/body/eval_jaxpr/ppermute | solution.py:13
  239.3 2.9 %fusion.46 = f32[1,8,8,1024]{3,2,1,0:T(8,128)} fusion(f32[8,8,1024]{2,1,0:T(8,128)S(1)} %get-tuple-element.181, f32[64,1024]{1,0:T(8,128)} %fusion.25, f32[64,1024]{1,0:T(8,128)} %fusion.27, bf16[3,1024,1024]{2,1,0:T(8,128)(2,1)} %param.12, bf16[3,10,8,1024]{3,2,1,0:T(8,128)(2,1)} %copy-done.1, s32[]{:T(128)S(6)} %select_n.41, s32[]{:T(128)S(6)} %select_n.42), kind=kOutput, calls=%fused_computation.60 | convolution fusion | flops 134414336 | bytes 3276808 | tf_op jit(solution)/shard_map/dot_general | solution.py:86
  (299 shorter events, 33.5 us)
Async XLA Ops:
  6.5 47.1 %all-gather.2.cloned.1.call-start = ((), (), s32[]{:S(2)}) async-start(), calls=%async_computation | async-start | bytes 2228224 | tf_op jit(solution)/shard_map/all_gather | solution.py:67
  7.3 14.9 %collective-permute-start.1 = (bf16[1,8,8,1024]{3,2,1,0:T(8,128)(2,1)}, bf16[1,8,8,1024]{3,2,1,0:T(8,128)(2,1)S(1)}, u32[]{:S(2)}, u32[]{:S(2)}) collective-permute-start(bf16[1,8,8,1024]{3,2,1,0:T(8,128)(2,1)} %param.8), channel_id=1, source_target_pairs={{0,1},{1,2},{2,3},{3,4},{4,5},{5,6},{6,7},{7,8},{8,9},{9,10},{10,1... | collective-permute-start | bytes 393224 | tf_op jit(solution)/shard_map/ppermute | solution.py:21
  9.6 12.5 %collective-permute-start.2 = (bf16[1,8,8,1024]{3,2,1,0:T(8,128)(2,1)}, bf16[1,8,8,1024]{3,2,1,0:T(8,128)(2,1)S(1)}, u32[]{:S(2)}, u32[]{:S(2)}) collective-permute-start(bf16[1,8,8,1024]{3,2,1,0:T(8,128)(2,1)} %param.8), channel_id=1, source_target_pairs={{1,0},{2,1},{3,2},{4,3},{5,4},{6,5},{7,6},{8,7},{9,8},{10,9},{11,1... | collective-permute-start | bytes 393224 | tf_op jit(solution)/shard_map/ppermute | solution.py:24
  22.1 31.6 %copy-start = (bf16[2,15,48,1024]{3,2,1,0:T(8,128)(2,1)S(1)}, bf16[2,15,48,1024]{3,2,1,0:T(8,128)(2,1)}, u32[]{:S(2)}) copy-start(bf16[2,15,48,1024]{3,2,1,0:T(8,128)(2,1)} %param.10) | copy-start | bytes 8847364
  23.3 3.0 %copy-start.1 = (bf16[3,10,8,1024]{3,2,1,0:T(8,128)(2,1)}, bf16[3,10,8,1024]{3,2,1,0:T(8,128)(2,1)S(1)}, u32[]{:S(2)}) copy-start(bf16[3,10,8,1024]{3,2,1,0:T(8,128)(2,1)S(1)} %fusion.54) | copy-start | bytes 1474564
  57.0 5.9 %collective-permute-start = (f32[8,8,1024]{2,1,0:T(8,128)S(1)}, f32[8,8,1024]{2,1,0:T(8,128)S(1)}, u32[]{:S(2)}, u32[]{:S(2)}) collective-permute-start(f32[8,8,1024]{2,1,0:T(8,128)S(1)} %fusion.81), channel_id=1, source_target_pairs={{0,15},{1,0},{2,1},{3,2},{4,3},{5,4},{6,5},{7,6},{8,7},{9,8},{10,9... | collective-permute-start | bytes 786440 | tf_op jit(solution)/shard_map/while/body/eval_jaxpr/ppermute | solution.py:13
  66.1 8.5 %collective-permute-start = (f32[8,8,1024]{2,1,0:T(8,128)S(1)}, f32[8,8,1024]{2,1,0:T(8,128)S(1)}, u32[]{:S(2)}, u32[]{:S(2)}) collective-permute-start(f32[8,8,1024]{2,1,0:T(8,128)S(1)} %fusion.81), channel_id=1, source_target_pairs={{0,15},{1,0},{2,1},{3,2},{4,3},{5,4},{6,5},{7,6},{8,7},{9,8},{10,9... | collective-permute-start | bytes 786440 | tf_op jit(solution)/shard_map/while/body/eval_jaxpr/ppermute | solution.py:13
  77.8 8.5 %collective-permute-start = (f32[8,8,1024]{2,1,0:T(8,128)S(1)}, f32[8,8,1024]{2,1,0:T(8,128)S(1)}, u32[]{:S(2)}, u32[]{:S(2)}) collective-permute-start(f32[8,8,1024]{2,1,0:T(8,128)S(1)} %fusion.81), channel_id=1, source_target_pairs={{0,15},{1,0},{2,1},{3,2},{4,3},{5,4},{6,5},{7,6},{8,7},{9,8},{10,9... | collective-permute-start | bytes 786440 | tf_op jit(solution)/shard_map/while/body/eval_jaxpr/ppermute | solution.py:13
  89.6 8.5 %collective-permute-start = (f32[8,8,1024]{2,1,0:T(8,128)S(1)}, f32[8,8,1024]{2,1,0:T(8,128)S(1)}, u32[]{:S(2)}, u32[]{:S(2)}) collective-permute-start(f32[8,8,1024]{2,1,0:T(8,128)S(1)} %fusion.81), channel_id=1, source_target_pairs={{0,15},{1,0},{2,1},{3,2},{4,3},{5,4},{6,5},{7,6},{8,7},{9,8},{10,9... | collective-permute-start | bytes 786440 | tf_op jit(solution)/shard_map/while/body/eval_jaxpr/ppermute | solution.py:13
  101.4 8.5 %collective-permute-start = (f32[8,8,1024]{2,1,0:T(8,128)S(1)}, f32[8,8,1024]{2,1,0:T(8,128)S(1)}, u32[]{:S(2)}, u32[]{:S(2)}) collective-permute-start(f32[8,8,1024]{2,1,0:T(8,128)S(1)} %fusion.81), channel_id=1, source_target_pairs={{0,15},{1,0},{2,1},{3,2},{4,3},{5,4},{6,5},{7,6},{8,7},{9,8},{10,9... | collective-permute-start | bytes 786440 | tf_op jit(solution)/shard_map/while/body/eval_jaxpr/ppermute | solution.py:13
  113.1 8.5 %collective-permute-start = (f32[8,8,1024]{2,1,0:T(8,128)S(1)}, f32[8,8,1024]{2,1,0:T(8,128)S(1)}, u32[]{:S(2)}, u32[]{:S(2)}) collective-permute-start(f32[8,8,1024]{2,1,0:T(8,128)S(1)} %fusion.81), channel_id=1, source_target_pairs={{0,15},{1,0},{2,1},{3,2},{4,3},{5,4},{6,5},{7,6},{8,7},{9,8},{10,9... | collective-permute-start | bytes 786440 | tf_op jit(solution)/shard_map/while/body/eval_jaxpr/ppermute | solution.py:13
  124.9 8.5 %collective-permute-start = (f32[8,8,1024]{2,1,0:T(8,128)S(1)}, f32[8,8,1024]{2,1,0:T(8,128)S(1)}, u32[]{:S(2)}, u32[]{:S(2)}) collective-permute-start(f32[8,8,1024]{2,1,0:T(8,128)S(1)} %fusion.81), channel_id=1, source_target_pairs={{0,15},{1,0},{2,1},{3,2},{4,3},{5,4},{6,5},{7,6},{8,7},{9,8},{10,9... | collective-permute-start | bytes 786440 | tf_op jit(solution)/shard_map/while/body/eval_jaxpr/ppermute | solution.py:13
  136.6 8.5 %collective-permute-start = (f32[8,8,1024]{2,1,0:T(8,128)S(1)}, f32[8,8,1024]{2,1,0:T(8,128)S(1)}, u32[]{:S(2)}, u32[]{:S(2)}) collective-permute-start(f32[8,8,1024]{2,1,0:T(8,128)S(1)} %fusion.81), channel_id=1, source_target_pairs={{0,15},{1,0},{2,1},{3,2},{4,3},{5,4},{6,5},{7,6},{8,7},{9,8},{10,9... | collective-permute-start | bytes 786440 | tf_op jit(solution)/shard_map/while/body/eval_jaxpr/ppermute | solution.py:13
  148.4 8.5 %collective-permute-start = (f32[8,8,1024]{2,1,0:T(8,128)S(1)}, f32[8,8,1024]{2,1,0:T(8,128)S(1)}, u32[]{:S(2)}, u32[]{:S(2)}) collective-permute-start(f32[8,8,1024]{2,1,0:T(8,128)S(1)} %fusion.81), channel_id=1, source_target_pairs={{0,15},{1,0},{2,1},{3,2},{4,3},{5,4},{6,5},{7,6},{8,7},{9,8},{10,9... | collective-permute-start | bytes 786440 | tf_op jit(solution)/shard_map/while/body/eval_jaxpr/ppermute | solution.py:13
  160.2 8.5 %collective-permute-start = (f32[8,8,1024]{2,1,0:T(8,128)S(1)}, f32[8,8,1024]{2,1,0:T(8,128)S(1)}, u32[]{:S(2)}, u32[]{:S(2)}) collective-permute-start(f32[8,8,1024]{2,1,0:T(8,128)S(1)} %fusion.81), channel_id=1, source_target_pairs={{0,15},{1,0},{2,1},{3,2},{4,3},{5,4},{6,5},{7,6},{8,7},{9,8},{10,9... | collective-permute-start | bytes 786440 | tf_op jit(solution)/shard_map/while/body/eval_jaxpr/ppermute | solution.py:13
  171.9 8.5 %collective-permute-start = (f32[8,8,1024]{2,1,0:T(8,128)S(1)}, f32[8,8,1024]{2,1,0:T(8,128)S(1)}, u32[]{:S(2)}, u32[]{:S(2)}) collective-permute-start(f32[8,8,1024]{2,1,0:T(8,128)S(1)} %fusion.81), channel_id=1, source_target_pairs={{0,15},{1,0},{2,1},{3,2},{4,3},{5,4},{6,5},{7,6},{8,7},{9,8},{10,9... | collective-permute-start | bytes 786440 | tf_op jit(solution)/shard_map/while/body/eval_jaxpr/ppermute | solution.py:13
  183.7 8.5 %collective-permute-start = (f32[8,8,1024]{2,1,0:T(8,128)S(1)}, f32[8,8,1024]{2,1,0:T(8,128)S(1)}, u32[]{:S(2)}, u32[]{:S(2)}) collective-permute-start(f32[8,8,1024]{2,1,0:T(8,128)S(1)} %fusion.81), channel_id=1, source_target_pairs={{0,15},{1,0},{2,1},{3,2},{4,3},{5,4},{6,5},{7,6},{8,7},{9,8},{10,9... | collective-permute-start | bytes 786440 | tf_op jit(solution)/shard_map/while/body/eval_jaxpr/ppermute | solution.py:13
  195.5 8.5 %collective-permute-start = (f32[8,8,1024]{2,1,0:T(8,128)S(1)}, f32[8,8,1024]{2,1,0:T(8,128)S(1)}, u32[]{:S(2)}, u32[]{:S(2)}) collective-permute-start(f32[8,8,1024]{2,1,0:T(8,128)S(1)} %fusion.81), channel_id=1, source_target_pairs={{0,15},{1,0},{2,1},{3,2},{4,3},{5,4},{6,5},{7,6},{8,7},{9,8},{10,9... | collective-permute-start | bytes 786440 | tf_op jit(solution)/shard_map/while/body/eval_jaxpr/ppermute | solution.py:13
  207.2 8.5 %collective-permute-start = (f32[8,8,1024]{2,1,0:T(8,128)S(1)}, f32[8,8,1024]{2,1,0:T(8,128)S(1)}, u32[]{:S(2)}, u32[]{:S(2)}) collective-permute-start(f32[8,8,1024]{2,1,0:T(8,128)S(1)} %fusion.81), channel_id=1, source_target_pairs={{0,15},{1,0},{2,1},{3,2},{4,3},{5,4},{6,5},{7,6},{8,7},{9,8},{10,9... | collective-permute-start | bytes 786440 | tf_op jit(solution)/shard_map/while/body/eval_jaxpr/ppermute | solution.py:13
  219.0 8.5 %collective-permute-start = (f32[8,8,1024]{2,1,0:T(8,128)S(1)}, f32[8,8,1024]{2,1,0:T(8,128)S(1)}, u32[]{:S(2)}, u32[]{:S(2)}) collective-permute-start(f32[8,8,1024]{2,1,0:T(8,128)S(1)} %fusion.81), channel_id=1, source_target_pairs={{0,15},{1,0},{2,1},{3,2},{4,3},{5,4},{6,5},{7,6},{8,7},{9,8},{10,9... | collective-permute-start | bytes 786440 | tf_op jit(solution)/shard_map/while/body/eval_jaxpr/ppermute | solution.py:13
  230.8 8.5 %collective-permute-start = (f32[8,8,1024]{2,1,0:T(8,128)S(1)}, f32[8,8,1024]{2,1,0:T(8,128)S(1)}, u32[]{:S(2)}, u32[]{:S(2)}) collective-permute-start(f32[8,8,1024]{2,1,0:T(8,128)S(1)} %fusion.81), channel_id=1, source_target_pairs={{0,15},{1,0},{2,1},{3,2},{4,3},{5,4},{6,5},{7,6},{8,7},{9,8},{10,9... | collective-permute-start | bytes 786440 | tf_op jit(solution)/shard_map/while/body/eval_jaxpr/ppermute | solution.py:13
Sparse Core Ops, SparseCore 0:
  9.5 44.1 all-gather.1
where the time goes:
time: 250 us; the launch traced here: 249 us
  waiting for transfers between devices  87.6 us (35%)
  starting transfers between devices  75.5 us (30%)
  matrix products  55.8 us (22%)
  between operations  20.8 us (8%)
  local copies, waits for them, and re-layouts  6.14 us (2%)
    ppermute x16, starting transfers between devices, from_behind(): lax.ppermute(value, axis, [(i, (i + by) % count) for i in range(count)])  71.9 us
    ppermute x16, waiting for transfers between devices, from_behind(): lax.ppermute(value, axis, [(i, (i + by) % count) for i in range(count)])  62.2 us
    dot_general x16, matrix products, far_term(): jnp.einsum('sbn,krn->skbr', source_row, left, preferred_element_type=jnp....  37.4 us
    all_gather x1, waiting for transfers between devices, local(): gathered = lax.all_gather(sources, 'row', axis=0, tiled=True)  24.7 us
    dot_general x16, matrix products, far_term(): jnp.einsum('jkbr,krn->jbn', spread(coeffs), right, preferred_element_type...  9.73 us
    dot_general x3, matrix products, local(): jnp.dot(shifted.reshape(-1, width), near_blocks[index], preferred_element...  8.65 us
  transfers between devices with their start and end apart: 19, of which 17 were waited for; matrix products, arithmetic and copies ran while one was open for 4% of the time, Pallas kernels for 0%

commit v1 on v0

--- a/solution.py
+++ b/solution.py
@@ -64,7 +64,23 @@
         keep = lax.dynamic_index_in_dim(keep_all, wrap_bit, 0, keepdims=False)
         return far_term(source_row, left, right, keep)
 
-    gathered = lax.all_gather(sources, "row", axis=0, tiled=True)
+    ways, here, step_2 = (lax.axis_size("row"), lax.axis_index("row"), sources.shape[0])
+    lengths = [n * ways if d == 0 else n for d, n in enumerate(sources.shape)]
+    full = lax.dynamic_update_slice_in_dim(
+        jnp.zeros(lengths, sources.dtype), sources, here * step_2, axis=0
+    )
+    going_up = going_down = sources
+    for far_2 in range(1, ways // 2 + 1):
+        going_up = lax.ppermute(going_up, "row", [(d, (d + 1) % ways) for d in range(ways)])
+        full = lax.dynamic_update_slice_in_dim(
+            full, going_up, (here - far_2) % ways * step_2, axis=0
+        )
+        if 2 * far_2 < ways:
+            going_down = lax.ppermute(going_down, "row", [(d, (d - 1) % ways) for d in range(ways)])
+            full = lax.dynamic_update_slice_in_dim(
+                full, going_down, (here + far_2) % ways * step_2, axis=0
+            )
+    gathered = full
 
     def step(source_index, accums):
         down_acc, up_acc = accums

time: 250 us -> 263 us (1.052)
  starting transfers between devices: 75.5 us -> 106 us
  between operations: 20.8 us -> 7.95 us
  waiting for transfers between devices: 87.6 us -> 81.7 us
  local copies, waits for them, and re-layouts: 6.14 us -> 8.8 us
    ppermute x0 -> x15, starting transfers between devices: none -> 33.2 us  [the longest x7 31.5 us: local(): lax.ppermute(going_down, 'row', [(d, (d - 1) % ways) for d in range(ways)])]
    all_gather x1 -> x0, waiting for transfers between devices: 24.7 us -> none  [local(): gathered = lax.all_gather(sources, 'row', axis=0, tiled=True)]
    ppermute x0 -> x15, waiting for transfers between devices: none -> 19.5 us  [the longest x8 10.5 us: local(): lax.ppermute(going_up, 'row', [(d, (d + 1) % ways) for d in range(ways)])]
  transfers between devices with their start and end apart: 19 -> 33, of which waited for: 17 -> 28; matrix products, arithmetic and copies ran while one was open for 4% -> 5% of each run, Pallas kernels for 0% -> 0%
where the time goes in v1:
time: 263 us; the launch traced here: 262 us
  starting transfers between devices  106 us (40%)
  waiting for transfers between devices  81.7 us (31%)
  matrix products  54.1 us (21%)
  local copies, waits for them, and re-layouts  8.8 us (3%)
  between operations  7.95 us (3%)
    ppermute x16, starting transfers between devices, from_behind(): lax.ppermute(value, axis, [(i, (i + by) % count) for i in range(count)])  69.9 us
    ppermute x16, waiting for transfers between devices, from_behind(): lax.ppermute(value, axis, [(i, (i + by) % count) for i in range(count)])  62.2 us
    dot_general x16, matrix products, far_term(): jnp.einsum('sbn,krn->skbr', source_row, left, preferred_element_type=jnp....  37.4 us
    ppermute x7, starting transfers between devices, local(): lax.ppermute(going_down, 'row', [(d, (d - 1) % ways) for d in range(ways)])  31.5 us
    ppermute x8, waiting for transfers between devices, local(): lax.ppermute(going_up, 'row', [(d, (d + 1) % ways) for d in range(ways)])  10.5 us
    dot_general x16, matrix products, far_term(): jnp.einsum('jkbr,krn->jbn', spread(coeffs), right, preferred_element_type...  9.75 us
    ppermute x7, waiting for transfers between devices, local(): lax.ppermute(going_down, 'row', [(d, (d - 1) % ways) for d in range(ways)])  9 us
    dot_general x3, matrix products, local(): jnp.dot(shifted.reshape(-1, width), near_blocks[index], preferred_element...  6.92 us
  transfers between devices with their start and end apart: 33, of which 28 were waited for; matrix products, arithmetic and copies ran while one was open for 5% of the time, Pallas kernels for 0%

profile of v1, /device:TPU:0, one launch (start us, length us, event | category | flops | bytes accessed | tf_op | source)
XLA Modules:
  0.0 262.0 jit_solution(9330645696975670146)
XLA Ops:
  0.5 5.0 %collective-permute-start.4 = (bf16[1,8,8,1024]{3,2,1,0:T(8,128)(2,1)}, bf16[1,8,8,1024]{3,2,1,0:T(8,128)(2,1)S(1)}, u32[]{:S(2)}, u32[]{:S(2)}) collective-permute-start(bf16[1,8,8,1024]{3,2,1,0:T(8,128)(2,1)} %param.8), channel_id=1, source_target_pairs={{0,15},{1,0},{2,1},{3,2},{4,3},{5,4},{6,5},{7,6},{8,7},{9,8},{10,9... | collective-permute-start | bytes 393224 | tf_op jit(solution)/shard_map/ppermute | solution.py:79
  25.4 2.8 %fusion.40 = f32[8,8,1024]{2,1,0:T(8,128)} fusion(f32[64,1024]{1,0:T(8,128)S(1)} %fusion.25, f32[64,1024]{1,0:T(8,128)S(1)} %fusion.27, bf16[3,1024,1024]{2,1,0:T(8,128)(2,1)} %param.12, bf16[3,10,8,1024]{3,2,1,0:T(8,128)(2,1)S(1)} %fusion.48, s32[]{:T(128)S(6)} %select_n.152, s32[]{:T(128)S(6)} %select_n.153), kind=kOutput, calls=%fused_computation.58 | convolution fusion | flops 134348800 | bytes 3014664 | tf_op jit(solution)/shard_map/dot_general | solution.py:102
  28.2 3.3 %collective-permute-start.6 = (bf16[1,8,8,1024]{3,2,1,0:T(8,128)(2,1)S(1)}, bf16[1,8,8,1024]{3,2,1,0:T(8,128)(2,1)S(1)}, u32[]{:S(2)}, u32[]{:S(2)}) collective-permute-start(bf16[1,8,8,1024]{3,2,1,0:T(8,128)(2,1)S(1)} %collective-permute-done.4), channel_id=1, source_target_pairs={{0,15},{1,0},{2,1},{3,2},{4,3},{5,4},{6,5},{7,6},{8,7},{9,8},{10,9... | collective-permute-start | bytes 393224 | tf_op jit(solution)/shard_map/ppermute | solution.py:79
  34.0 4.7 %collective-permute-start.8 = (bf16[1,8,8,1024]{3,2,1,0:T(8,128)(2,1)S(1)}, bf16[1,8,8,1024]{3,2,1,0:T(8,128)(2,1)S(1)}, u32[]{:S(2)}, u32[]{:S(2)}) collective-permute-start(bf16[1,8,8,1024]{3,2,1,0:T(8,128)(2,1)S(1)} %collective-permute-done.6), channel_id=1, source_target_pairs={{0,15},{1,0},{2,1},{3,2},{4,3},{5,4},{6,5},{7,6},{8,7},{9,8},{10,9... | collective-permute-start | bytes 393224 | tf_op jit(solution)/shard_map/ppermute | solution.py:79
  41.2 4.6 %collective-permute-start.10 = (bf16[1,8,8,1024]{3,2,1,0:T(8,128)(2,1)S(1)}, bf16[1,8,8,1024]{3,2,1,0:T(8,128)(2,1)S(1)}, u32[]{:S(2)}, u32[]{:S(2)}) collective-permute-start(bf16[1,8,8,1024]{3,2,1,0:T(8,128)(2,1)S(1)} %collective-permute-done.8), channel_id=1, source_target_pairs={{0,15},{1,0},{2,1},{3,2},{4,3},{5,4},{6,5},{7,6},{8,7},{9,8},{10,9... | collective-permute-start | bytes 393224 | tf_op jit(solution)/shard_map/ppermute | solution.py:79
  48.3 4.6 %collective-permute-start.12 = (bf16[1,8,8,1024]{3,2,1,0:T(8,128)(2,1)S(1)}, bf16[1,8,8,1024]{3,2,1,0:T(8,128)(2,1)S(1)}, u32[]{:S(2)}, u32[]{:S(2)}) collective-permute-start(bf16[1,8,8,1024]{3,2,1,0:T(8,128)(2,1)S(1)} %collective-permute-done.10), channel_id=1, source_target_pairs={{0,15},{1,0},{2,1},{3,2},{4,3},{5,4},{6,5},{7,6},{8,7},{9,8},{10,9... | collective-permute-start | bytes 393224 | tf_op jit(solution)/shard_map/ppermute | solution.py:79
  55.5 4.7 %collective-permute-start.14 = (bf16[1,8,8,1024]{3,2,1,0:T(8,128)(2,1)S(1)}, bf16[1,8,8,1024]{3,2,1,0:T(8,128)(2,1)S(1)}, u32[]{:S(2)}, u32[]{:S(2)}) collective-permute-start(bf16[1,8,8,1024]{3,2,1,0:T(8,128)(2,1)S(1)} %collective-permute-done.12), channel_id=1, source_target_pairs={{0,15},{1,0},{2,1},{3,2},{4,3},{5,4},{6,5},{7,6},{8,7},{9,8},{10,9... | collective-permute-start | bytes 393224 | tf_op jit(solution)/shard_map/ppermute | solution.py:79
  62.7 4.6 %collective-permute-start.16 = (bf16[1,8,8,1024]{3,2,1,0:T(8,128)(2,1)S(1)}, bf16[1,8,8,1024]{3,2,1,0:T(8,128)(2,1)S(1)}, u32[]{:S(2)}, u32[]{:S(2)}) collective-permute-start(bf16[1,8,8,1024]{3,2,1,0:T(8,128)(2,1)S(1)} %collective-permute-done.14), channel_id=1, source_target_pairs={{0,15},{1,0},{2,1},{3,2},{4,3},{5,4},{6,5},{7,6},{8,7},{9,8},{10,9... | collective-permute-start | bytes 393224 | tf_op jit(solution)/shard_map/ppermute | solution.py:79
  69.8 5.6 %collective-permute-done.17 = bf16[1,8,8,1024]{3,2,1,0:T(8,128)(2,1)S(1)} collective-permute-done((bf16[1,8,8,1024]{3,2,1,0:T(8,128)(2,1)S(1)}, bf16[1,8,8,1024]{3,2,1,0:T(8,128)(2,1)S(1)}, u32[]{:S(2)}, u32[]{:S(2)}) %collective-permute-start.17) | collective-permute-done | bytes 131104 | tf_op jit(solution)/shard_map/ppermute | solution.py:74
  76.7 183.6 %while.15 = (s32[]{:T(128)}, f32[8,8,1024]{2,1,0:T(8,128)S(1)}, s32[]{:T(128)}, bf16[2,15,48,1024]{3,2,1,0:T(8,128)(2,1)}, bf16[16,8,8,1024]{3,2,1,0:T(8,128)(2,...) while((s32[]{:T(128)}, f32[8,8,1024]{2,1,0:T(8,128)S(1)}, ...), condition=%wide.region_3.4_spmd, body=%wide.region_2.3_spmd.sunk | while | flops 188901376 | bytes 8549533 | solution.py:93
  76.7 2.3 fusion.74
  80.0 3.9 %collective-permute-done = f32[8,8,1024]{2,1,0:T(8,128)S(1)} collective-permute-done((f32[8,8,1024]{2,1,0:T(8,128)S(1)}, f32[8,8,1024]{2,1,0:T(8,128)S(1)}, u32[]{:S(2)}, u32[]{:S(2)}) %collective-permute-start) | collective-permute-done | bytes 262176 | tf_op jit(solution)/shard_map/while/body/eval_jaxpr/ppermute | solution.py:13
  87.1 4.7 %collective-permute-start = (f32[8,8,1024]{2,1,0:T(8,128)S(1)}, f32[8,8,1024]{2,1,0:T(8,128)S(1)}, u32[]{:S(2)}, u32[]{:S(2)}) collective-permute-start(f32[8,8,1024]{2,1,0:T(8,128)S(1)} %fusion.75), channel_id=1, source_target_pairs={{0,15},{1,0},{2,1},{3,2},{4,3},{5,4},{6,5},{7,6},{8,7},{9,8},{10,9... | collective-permute-start | bytes 786440 | tf_op jit(solution)/shard_map/while/body/eval_jaxpr/ppermute | solution.py:13
  91.8 3.9 %collective-permute-done = f32[8,8,1024]{2,1,0:T(8,128)S(1)} collective-permute-done((f32[8,8,1024]{2,1,0:T(8,128)S(1)}, f32[8,8,1024]{2,1,0:T(8,128)S(1)}, u32[]{:S(2)}, u32[]{:S(2)}) %collective-permute-start) | collective-permute-done | bytes 262176 | tf_op jit(solution)/shard_map/while/body/eval_jaxpr/ppermute | solution.py:13
  98.9 4.7 %collective-permute-start = (f32[8,8,1024]{2,1,0:T(8,128)S(1)}, f32[8,8,1024]{2,1,0:T(8,128)S(1)}, u32[]{:S(2)}, u32[]{:S(2)}) collective-permute-start(f32[8,8,1024]{2,1,0:T(8,128)S(1)} %fusion.75), channel_id=1, source_target_pairs={{0,15},{1,0},{2,1},{3,2},{4,3},{5,4},{6,5},{7,6},{8,7},{9,8},{10,9... | collective-permute-start | bytes 786440 | tf_op jit(solution)/shard_map/while/body/eval_jaxpr/ppermute | solution.py:13
  103.5 3.9 %collective-permute-done = f32[8,8,1024]{2,1,0:T(8,128)S(1)} collective-permute-done((f32[8,8,1024]{2,1,0:T(8,128)S(1)}, f32[8,8,1024]{2,1,0:T(8,128)S(1)}, u32[]{:S(2)}, u32[]{:S(2)}) %collective-permute-start) | collective-permute-done | bytes 262176 | tf_op jit(solution)/shard_map/while/body/eval_jaxpr/ppermute | solution.py:13
  110.6 4.7 %collective-permute-start = (f32[8,8,1024]{2,1,0:T(8,128)S(1)}, f32[8,8,1024]{2,1,0:T(8,128)S(1)}, u32[]{:S(2)}, u32[]{:S(2)}) collective-permute-start(f32[8,8,1024]{2,1,0:T(8,128)S(1)} %fusion.75), channel_id=1, source_target_pairs={{0,15},{1,0},{2,1},{3,2},{4,3},{5,4},{6,5},{7,6},{8,7},{9,8},{10,9... | collective-permute-start | bytes 786440 | tf_op jit(solution)/shard_map/while/body/eval_jaxpr/ppermute | solution.py:13
  115.3 3.9 %collective-permute-done = f32[8,8,1024]{2,1,0:T(8,128)S(1)} collective-permute-done((f32[8,8,1024]{2,1,0:T(8,128)S(1)}, f32[8,8,1024]{2,1,0:T(8,128)S(1)}, u32[]{:S(2)}, u32[]{:S(2)}) %collective-permute-start) | collective-permute-done | bytes 262176 | tf_op jit(solution)/shard_map/while/body/eval_jaxpr/ppermute | solution.py:13
  122.4 4.7 %collective-permute-start = (f32[8,8,1024]{2,1,0:T(8,128)S(1)}, f32[8,8,1024]{2,1,0:T(8,128)S(1)}, u32[]{:S(2)}, u32[]{:S(2)}) collective-permute-start(f32[8,8,1024]{2,1,0:T(8,128)S(1)} %fusion.75), channel_id=1, source_target_pairs={{0,15},{1,0},{2,1},{3,2},{4,3},{5,4},{6,5},{7,6},{8,7},{9,8},{10,9... | collective-permute-start | bytes 786440 | tf_op jit(solution)/shard_map/while/body/eval_jaxpr/ppermute | solution.py:13
  127.1 3.9 %collective-permute-done = f32[8,8,1024]{2,1,0:T(8,128)S(1)} collective-permute-done((f32[8,8,1024]{2,1,0:T(8,128)S(1)}, f32[8,8,1024]{2,1,0:T(8,128)S(1)}, u32[]{:S(2)}, u32[]{:S(2)}) %collective-permute-start) | collective-permute-done | bytes 262176 | tf_op jit(solution)/shard_map/while/body/eval_jaxpr/ppermute | solution.py:13
  131.0 2.3 fusion.74
  134.2 4.7 %collective-permute-start = (f32[8,8,1024]{2,1,0:T(8,128)S(1)}, f32[8,8,1024]{2,1,0:T(8,128)S(1)}, u32[]{:S(2)}, u32[]{:S(2)}) collective-permute-start(f32[8,8,1024]{2,1,0:T(8,128)S(1)} %fusion.75), channel_id=1, source_target_pairs={{0,15},{1,0},{2,1},{3,2},{4,3},{5,4},{6,5},{7,6},{8,7},{9,8},{10,9... | collective-permute-start | bytes 786440 | tf_op jit(solution)/shard_map/while/body/eval_jaxpr/ppermute | solution.py:13
  138.8 3.9 %collective-permute-done = f32[8,8,1024]{2,1,0:T(8,128)S(1)} collective-permute-done((f32[8,8,1024]{2,1,0:T(8,128)S(1)}, f32[8,8,1024]{2,1,0:T(8,128)S(1)}, u32[]{:S(2)}, u32[]{:S(2)}) %collective-permute-start) | collective-permute-done | bytes 262176 | tf_op jit(solution)/shard_map/while/body/eval_jaxpr/ppermute | solution.py:13
  145.9 4.7 %collective-permute-start = (f32[8,8,1024]{2,1,0:T(8,128)S(1)}, f32[8,8,1024]{2,1,0:T(8,128)S(1)}, u32[]{:S(2)}, u32[]{:S(2)}) collective-permute-start(f32[8,8,1024]{2,1,0:T(8,128)S(1)} %fusion.75), channel_id=1, source_target_pairs={{0,15},{1,0},{2,1},{3,2},{4,3},{5,4},{6,5},{7,6},{8,7},{9,8},{10,9... | collective-permute-start | bytes 786440 | tf_op jit(solution)/shard_map/while/body/eval_jaxpr/ppermute | solution.py:13
  150.6 3.9 %collective-permute-done = f32[8,8,1024]{2,1,0:T(8,128)S(1)} collective-permute-done((f32[8,8,1024]{2,1,0:T(8,128)S(1)}, f32[8,8,1024]{2,1,0:T(8,128)S(1)}, u32[]{:S(2)}, u32[]{:S(2)}) %collective-permute-start) | collective-permute-done | bytes 262176 | tf_op jit(solution)/shard_map/while/body/eval_jaxpr/ppermute | solution.py:13
  154.5 2.3 fusion.74
  157.7 4.7 %collective-permute-start = (f32[8,8,1024]{2,1,0:T(8,128)S(1)}, f32[8,8,1024]{2,1,0:T(8,128)S(1)}, u32[]{:S(2)}, u32[]{:S(2)}) collective-permute-start(f32[8,8,1024]{2,1,0:T(8,128)S(1)} %fusion.75), channel_id=1, source_target_pairs={{0,15},{1,0},{2,1},{3,2},{4,3},{5,4},{6,5},{7,6},{8,7},{9,8},{10,9... | collective-permute-start | bytes 786440 | tf_op jit(solution)/shard_map/while/body/eval_jaxpr/ppermute | solution.py:13
  162.4 3.9 %collective-permute-done = f32[8,8,1024]{2,1,0:T(8,128)S(1)} collective-permute-done((f32[8,8,1024]{2,1,0:T(8,128)S(1)}, f32[8,8,1024]{2,1,0:T(8,128)S(1)}, u32[]{:S(2)}, u32[]{:S(2)}) %collective-permute-start) | collective-permute-done | bytes 262176 | tf_op jit(solution)/shard_map/while/body/eval_jaxpr/ppermute | solution.py:13
  169.5 4.7 %collective-permute-start = (f32[8,8,1024]{2,1,0:T(8,128)S(1)}, f32[8,8,1024]{2,1,0:T(8,128)S(1)}, u32[]{:S(2)}, u32[]{:S(2)}) collective-permute-start(f32[8,8,1024]{2,1,0:T(8,128)S(1)} %fusion.75), channel_id=1, source_target_pairs={{0,15},{1,0},{2,1},{3,2},{4,3},{5,4},{6,5},{7,6},{8,7},{9,8},{10,9... | collective-permute-start | bytes 786440 | tf_op jit(solution)/shard_map/while/body/eval_jaxpr/ppermute | solution.py:13
  174.1 3.9 %collective-permute-done = f32[8,8,1024]{2,1,0:T(8,128)S(1)} collective-permute-done((f32[8,8,1024]{2,1,0:T(8,128)S(1)}, f32[8,8,1024]{2,1,0:T(8,128)S(1)}, u32[]{:S(2)}, u32[]{:S(2)}) %collective-permute-start) | collective-permute-done | bytes 262176 | tf_op jit(solution)/shard_map/while/body/eval_jaxpr/ppermute | solution.py:13
  178.0 2.3 fusion.74
  181.2 4.7 %collective-permute-start = (f32[8,8,1024]{2,1,0:T(8,128)S(1)}, f32[8,8,1024]{2,1,0:T(8,128)S(1)}, u32[]{:S(2)}, u32[]{:S(2)}) collective-permute-start(f32[8,8,1024]{2,1,0:T(8,128)S(1)} %fusion.75), channel_id=1, source_target_pairs={{0,15},{1,0},{2,1},{3,2},{4,3},{5,4},{6,5},{7,6},{8,7},{9,8},{10,9... | collective-permute-start | bytes 786440 | tf_op jit(solution)/shard_map/while/body/eval_jaxpr/ppermute | solution.py:13
  185.9 3.9 %collective-permute-done = f32[8,8,1024]{2,1,0:T(8,128)S(1)} collective-permute-done((f32[8,8,1024]{2,1,0:T(8,128)S(1)}, f32[8,8,1024]{2,1,0:T(8,128)S(1)}, u32[]{:S(2)}, u32[]{:S(2)}) %collective-permute-start) | collective-permute-done | bytes 262176 | tf_op jit(solution)/shard_map/while/body/eval_jaxpr/ppermute | solution.py:13
  193.0 4.7 %collective-permute-start = (f32[8,8,1024]{2,1,0:T(8,128)S(1)}, f32[8,8,1024]{2,1,0:T(8,128)S(1)}, u32[]{:S(2)}, u32[]{:S(2)}) collective-permute-start(f32[8,8,1024]{2,1,0:T(8,128)S(1)} %fusion.75), channel_id=1, source_target_pairs={{0,15},{1,0},{2,1},{3,2},{4,3},{5,4},{6,5},{7,6},{8,7},{9,8},{10,9... | collective-permute-start | bytes 786440 | tf_op jit(solution)/shard_map/while/body/eval_jaxpr/ppermute | solution.py:13
  197.6 3.9 %collective-permute-done = f32[8,8,1024]{2,1,0:T(8,128)S(1)} collective-permute-done((f32[8,8,1024]{2,1,0:T(8,128)S(1)}, f32[8,8,1024]{2,1,0:T(8,128)S(1)}, u32[]{:S(2)}, u32[]{:S(2)}) %collective-permute-start) | collective-permute-done | bytes 262176 | tf_op jit(solution)/shard_map/while/body/eval_jaxpr/ppermute | solution.py:13
  201.5 2.3 fusion.74
  204.8 4.7 %collective-permute-start = (f32[8,8,1024]{2,1,0:T(8,128)S(1)}, f32[8,8,1024]{2,1,0:T(8,128)S(1)}, u32[]{:S(2)}, u32[]{:S(2)}) collective-permute-start(f32[8,8,1024]{2,1,0:T(8,128)S(1)} %fusion.75), channel_id=1, source_target_pairs={{0,15},{1,0},{2,1},{3,2},{4,3},{5,4},{6,5},{7,6},{8,7},{9,8},{10,9... | collective-permute-start | bytes 786440 | tf_op jit(solution)/shard_map/while/body/eval_jaxpr/ppermute | solution.py:13
  209.4 3.9 %collective-permute-done = f32[8,8,1024]{2,1,0:T(8,128)S(1)} collective-permute-done((f32[8,8,1024]{2,1,0:T(8,128)S(1)}, f32[8,8,1024]{2,1,0:T(8,128)S(1)}, u32[]{:S(2)}, u32[]{:S(2)}) %collective-permute-start) | collective-permute-done | bytes 262176 | tf_op jit(solution)/shard_map/while/body/eval_jaxpr/ppermute | solution.py:13
  216.5 4.7 %collective-permute-start = (f32[8,8,1024]{2,1,0:T(8,128)S(1)}, f32[8,8,1024]{2,1,0:T(8,128)S(1)}, u32[]{:S(2)}, u32[]{:S(2)}) collective-permute-start(f32[8,8,1024]{2,1,0:T(8,128)S(1)} %fusion.75), channel_id=1, source_target_pairs={{0,15},{1,0},{2,1},{3,2},{4,3},{5,4},{6,5},{7,6},{8,7},{9,8},{10,9... | collective-permute-start | bytes 786440 | tf_op jit(solution)/shard_map/while/body/eval_jaxpr/ppermute | solution.py:13
  221.2 3.9 %collective-permute-done = f32[8,8,1024]{2,1,0:T(8,128)S(1)} collective-permute-done((f32[8,8,1024]{2,1,0:T(8,128)S(1)}, f32[8,8,1024]{2,1,0:T(8,128)S(1)}, u32[]{:S(2)}, u32[]{:S(2)}) %collective-permute-start) | collective-permute-done | bytes 262176 | tf_op jit(solution)/shard_map/while/body/eval_jaxpr/ppermute | solution.py:13
  225.1 2.3 fusion.74
  228.3 4.7 %collective-permute-start = (f32[8,8,1024]{2,1,0:T(8,128)S(1)}, f32[8,8,1024]{2,1,0:T(8,128)S(1)}, u32[]{:S(2)}, u32[]{:S(2)}) collective-permute-start(f32[8,8,1024]{2,1,0:T(8,128)S(1)} %fusion.75), channel_id=1, source_target_pairs={{0,15},{1,0},{2,1},{3,2},{4,3},{5,4},{6,5},{7,6},{8,7},{9,8},{10,9... | collective-permute-start | bytes 786440 | tf_op jit(solution)/shard_map/while/body/eval_jaxpr/ppermute | solution.py:13
  232.9 3.9 %collective-permute-done = f32[8,8,1024]{2,1,0:T(8,128)S(1)} collective-permute-done((f32[8,8,1024]{2,1,0:T(8,128)S(1)}, f32[8,8,1024]{2,1,0:T(8,128)S(1)}, u32[]{:S(2)}, u32[]{:S(2)}) %collective-permute-start) | collective-permute-done | bytes 262176 | tf_op jit(solution)/shard_map/while/body/eval_jaxpr/ppermute | solution.py:13
  240.0 4.7 %collective-permute-start = (f32[8,8,1024]{2,1,0:T(8,128)S(1)}, f32[8,8,1024]{2,1,0:T(8,128)S(1)}, u32[]{:S(2)}, u32[]{:S(2)}) collective-permute-start(f32[8,8,1024]{2,1,0:T(8,128)S(1)} %fusion.75), channel_id=1, source_target_pairs={{0,15},{1,0},{2,1},{3,2},{4,3},{5,4},{6,5},{7,6},{8,7},{9,8},{10,9... | collective-permute-start | bytes 786440 | tf_op jit(solution)/shard_map/while/body/eval_jaxpr/ppermute | solution.py:13
  244.7 3.9 %collective-permute-done = f32[8,8,1024]{2,1,0:T(8,128)S(1)} collective-permute-done((f32[8,8,1024]{2,1,0:T(8,128)S(1)}, f32[8,8,1024]{2,1,0:T(8,128)S(1)}, u32[]{:S(2)}, u32[]{:S(2)}) %collective-permute-start) | collective-permute-done | bytes 262176 | tf_op jit(solution)/shard_map/while/body/eval_jaxpr/ppermute | solution.py:13
  248.6 2.3 fusion.74
  251.8 4.7 %collective-permute-start = (f32[8,8,1024]{2,1,0:T(8,128)S(1)}, f32[8,8,1024]{2,1,0:T(8,128)S(1)}, u32[]{:S(2)}, u32[]{:S(2)}) collective-permute-start(f32[8,8,1024]{2,1,0:T(8,128)S(1)} %fusion.75), channel_id=1, source_target_pairs={{0,15},{1,0},{2,1},{3,2},{4,3},{5,4},{6,5},{7,6},{8,7},{9,8},{10,9... | collective-permute-start | bytes 786440 | tf_op jit(solution)/shard_map/while/body/eval_jaxpr/ppermute | solution.py:13
  256.5 3.9 %collective-permute-done = f32[8,8,1024]{2,1,0:T(8,128)S(1)} collective-permute-done((f32[8,8,1024]{2,1,0:T(8,128)S(1)}, f32[8,8,1024]{2,1,0:T(8,128)S(1)}, u32[]{:S(2)}, u32[]{:S(2)}) %collective-permute-start) | collective-permute-done | bytes 262176 | tf_op jit(solution)/shard_map/while/body/eval_jaxpr/ppermute | solution.py:13
  (346 shorter events, 64.6 us)
Async XLA Ops:
  0.0 20.0 %copy-start.2 = (bf16[1,8,8,1024]{3,2,1,0:T(8,128)(2,1)S(1)}, bf16[1,8,8,1024]{3,2,1,0:T(8,128)(2,1)}, u32[]{:S(2)}) copy-start(bf16[1,8,8,1024]{3,2,1,0:T(8,128)(2,1)} %param.8) | copy-start | bytes 393220
  0.0 24.2 %collective-permute-start.3 = (bf16[1,8,8,1024]{3,2,1,0:T(8,128)(2,1)}, bf16[1,8,8,1024]{3,2,1,0:T(8,128)(2,1)}, u32[]{:S(2)}, u32[]{:S(2)}) collective-permute-start(bf16[1,8,8,1024]{3,2,1,0:T(8,128)(2,1)} %param.8), channel_id=1, source_target_pairs={{0,1},{1,2},{2,3},{3,4},{4,5},{5,6},{6,7},{7,8},{8,9},{9,10},{10,1... | collective-permute-start | bytes 393224 | tf_op jit(solution)/shard_map/ppermute | solution.py:74
  0.5 27.7 %collective-permute-start.4 = (bf16[1,8,8,1024]{3,2,1,0:T(8,128)(2,1)}, bf16[1,8,8,1024]{3,2,1,0:T(8,128)(2,1)S(1)}, u32[]{:S(2)}, u32[]{:S(2)}) collective-permute-start(bf16[1,8,8,1024]{3,2,1,0:T(8,128)(2,1)} %param.8), channel_id=1, source_target_pairs={{0,15},{1,0},{2,1},{3,2},{4,3},{5,4},{6,5},{7,6},{8,7},{9,8},{10,9... | collective-permute-start | bytes 393224 | tf_op jit(solution)/shard_map/ppermute | solution.py:79
  5.5 14.5 %collective-permute-start.1 = (bf16[1,8,8,1024]{3,2,1,0:T(8,128)(2,1)}, bf16[1,8,8,1024]{3,2,1,0:T(8,128)(2,1)S(1)}, u32[]{:S(2)}, u32[]{:S(2)}) collective-permute-start(bf16[1,8,8,1024]{3,2,1,0:T(8,128)(2,1)} %param.8), channel_id=1, source_target_pairs={{0,1},{1,2},{2,3},{3,4},{4,5},{5,6},{6,7},{7,8},{8,9},{9,10},{10,1... | collective-permute-start | bytes 393224 | tf_op jit(solution)/shard_map/ppermute | solution.py:21
  6.8 13.2 %collective-permute-start.2 = (bf16[1,8,8,1024]{3,2,1,0:T(8,128)(2,1)}, bf16[1,8,8,1024]{3,2,1,0:T(8,128)(2,1)S(1)}, u32[]{:S(2)}, u32[]{:S(2)}) collective-permute-start(bf16[1,8,8,1024]{3,2,1,0:T(8,128)(2,1)} %param.8), channel_id=1, source_target_pairs={{1,0},{2,1},{3,2},{4,3},{5,4},{6,5},{7,6},{8,7},{9,8},{10,9},{11,1... | collective-permute-start | bytes 393224 | tf_op jit(solution)/shard_map/ppermute | solution.py:24
  24.2 8.2 %collective-permute-start.5 = (bf16[1,8,8,1024]{3,2,1,0:T(8,128)(2,1)}, bf16[1,8,8,1024]{3,2,1,0:T(8,128)(2,1)S(1)}, u32[]{:S(2)}, u32[]{:S(2)}) collective-permute-start(bf16[1,8,8,1024]{3,2,1,0:T(8,128)(2,1)} %collective-permute-done.3), channel_id=1, source_target_pairs={{0,1},{1,2},{2,3},{3,4},{4,5},{5,6},{6,7},{7,8},{8,9},{9,10},{10,1... | collective-permute-start | bytes 393224 | tf_op jit(solution)/shard_map/ppermute | solution.py:74
  28.2 48.5 %copy-start = (bf16[2,15,48,1024]{3,2,1,0:T(8,128)(2,1)S(1)}, bf16[2,15,48,1024]{3,2,1,0:T(8,128)(2,1)}, u32[]{:S(2)}) copy-start(bf16[2,15,48,1024]{3,2,1,0:T(8,128)(2,1)} %param.10) | copy-start | bytes 8847364
  28.2 5.8 %collective-permute-start.6 = (bf16[1,8,8,1024]{3,2,1,0:T(8,128)(2,1)S(1)}, bf16[1,8,8,1024]{3,2,1,0:T(8,128)(2,1)S(1)}, u32[]{:S(2)}, u32[]{:S(2)}) collective-permute-start(bf16[1,8,8,1024]{3,2,1,0:T(8,128)(2,1)S(1)} %collective-permute-done.4), channel_id=1, source_target_pairs={{0,15},{1,0},{2,1},{3,2},{4,3},{5,4},{6,5},{7,6},{8,7},{9,8},{10,9... | collective-permute-start | bytes 393224 | tf_op jit(solution)/shard_map/ppermute | solution.py:79
  32.5 7.2 %collective-permute-start.7 = (bf16[1,8,8,1024]{3,2,1,0:T(8,128)(2,1)S(1)}, bf16[1,8,8,1024]{3,2,1,0:T(8,128)(2,1)S(1)}, u32[]{:S(2)}, u32[]{:S(2)}) collective-permute-start(bf16[1,8,8,1024]{3,2,1,0:T(8,128)(2,1)S(1)} %collective-permute-done.5), channel_id=1, source_target_pairs={{0,1},{1,2},{2,3},{3,4},{4,5},{5,6},{6,7},{7,8},{8,9},{9,10},{10,1... | collective-permute-start | bytes 393224 | tf_op jit(solution)/shard_map/ppermute | solution.py:74
  34.0 7.2 %collective-permute-start.8 = (bf16[1,8,8,1024]{3,2,1,0:T(8,128)(2,1)S(1)}, bf16[1,8,8,1024]{3,2,1,0:T(8,128)(2,1)S(1)}, u32[]{:S(2)}, u32[]{:S(2)}) collective-permute-start(bf16[1,8,8,1024]{3,2,1,0:T(8,128)(2,1)S(1)} %collective-permute-done.6), channel_id=1, source_target_pairs={{0,15},{1,0},{2,1},{3,2},{4,3},{5,4},{6,5},{7,6},{8,7},{9,8},{10,9... | collective-permute-start | bytes 393224 | tf_op jit(solution)/shard_map/ppermute | solution.py:79
  39.7 7.1 %collective-permute-start.9 = (bf16[1,8,8,1024]{3,2,1,0:T(8,128)(2,1)S(1)}, bf16[1,8,8,1024]{3,2,1,0:T(8,128)(2,1)S(1)}, u32[]{:S(2)}, u32[]{:S(2)}) collective-permute-start(bf16[1,8,8,1024]{3,2,1,0:T(8,128)(2,1)S(1)} %collective-permute-done.7), channel_id=1, source_target_pairs={{0,1},{1,2},{2,3},{3,4},{4,5},{5,6},{6,7},{7,8},{8,9},{9,10},{10,1... | collective-permute-start | bytes 393224 | tf_op jit(solution)/shard_map/ppermute | solution.py:74
  41.2 7.1 %collective-permute-start.10 = (bf16[1,8,8,1024]{3,2,1,0:T(8,128)(2,1)S(1)}, bf16[1,8,8,1024]{3,2,1,0:T(8,128)(2,1)S(1)}, u32[]{:S(2)}, u32[]{:S(2)}) collective-permute-start(bf16[1,8,8,1024]{3,2,1,0:T(8,128)(2,1)S(1)} %collective-permute-done.8), channel_id=1, source_target_pairs={{0,15},{1,0},{2,1},{3,2},{4,3},{5,4},{6,5},{7,6},{8,7},{9,8},{10,9... | collective-permute-start | bytes 393224 | tf_op jit(solution)/shard_map/ppermute | solution.py:79
  46.8 7.2 %collective-permute-start.11 = (bf16[1,8,8,1024]{3,2,1,0:T(8,128)(2,1)S(1)}, bf16[1,8,8,1024]{3,2,1,0:T(8,128)(2,1)S(1)}, u32[]{:S(2)}, u32[]{:S(2)}) collective-permute-start(bf16[1,8,8,1024]{3,2,1,0:T(8,128)(2,1)S(1)} %collective-permute-done.9), channel_id=1, source_target_pairs={{0,1},{1,2},{2,3},{3,4},{4,5},{5,6},{6,7},{7,8},{8,9},{9,10},{10,1... | collective-permute-start | bytes 393224 | tf_op jit(solution)/shard_map/ppermute | solution.py:74
  48.3 7.2 %collective-permute-start.12 = (bf16[1,8,8,1024]{3,2,1,0:T(8,128)(2,1)S(1)}, bf16[1,8,8,1024]{3,2,1,0:T(8,128)(2,1)S(1)}, u32[]{:S(2)}, u32[]{:S(2)}) collective-permute-start(bf16[1,8,8,1024]{3,2,1,0:T(8,128)(2,1)S(1)} %collective-permute-done.10), channel_id=1, source_target_pairs={{0,15},{1,0},{2,1},{3,2},{4,3},{5,4},{6,5},{7,6},{8,7},{9,8},{10,9... | collective-permute-start | bytes 393224 | tf_op jit(solution)/shard_map/ppermute | solution.py:79
  54.0 7.2 %collective-permute-start.13 = (bf16[1,8,8,1024]{3,2,1,0:T(8,128)(2,1)S(1)}, bf16[1,8,8,1024]{3,2,1,0:T(8,128)(2,1)S(1)}, u32[]{:S(2)}, u32[]{:S(2)}) collective-permute-start(bf16[1,8,8,1024]{3,2,1,0:T(8,128)(2,1)S(1)} %collective-permute-done.11), channel_id=1, source_target_pairs={{0,1},{1,2},{2,3},{3,4},{4,5},{5,6},{6,7},{7,8},{8,9},{9,10},{10,1... | collective-permute-start | bytes 393224 | tf_op jit(solution)/shard_map/ppermute | solution.py:74
  55.5 7.2 %collective-permute-start.14 = (bf16[1,8,8,1024]{3,2,1,0:T(8,128)(2,1)S(1)}, bf16[1,8,8,1024]{3,2,1,0:T(8,128)(2,1)S(1)}, u32[]{:S(2)}, u32[]{:S(2)}) collective-permute-start(bf16[1,8,8,1024]{3,2,1,0:T(8,128)(2,1)S(1)} %collective-permute-done.12), channel_id=1, source_target_pairs={{0,15},{1,0},{2,1},{3,2},{4,3},{5,4},{6,5},{7,6},{8,7},{9,8},{10,9... | collective-permute-start | bytes 393224 | tf_op jit(solution)/shard_map/ppermute | solution.py:79
  61.2 7.1 %collective-permute-start.15 = (bf16[1,8,8,1024]{3,2,1,0:T(8,128)(2,1)S(1)}, bf16[1,8,8,1024]{3,2,1,0:T(8,128)(2,1)S(1)}, u32[]{:S(2)}, u32[]{:S(2)}) collective-permute-start(bf16[1,8,8,1024]{3,2,1,0:T(8,128)(2,1)S(1)} %collective-permute-done.13), channel_id=1, source_target_pairs={{0,1},{1,2},{2,3},{3,4},{4,5},{5,6},{6,7},{7,8},{8,9},{9,10},{10,1... | collective-permute-start | bytes 393224 | tf_op jit(solution)/shard_map/ppermute | solution.py:74
  62.7 7.1 %collective-permute-start.16 = (bf16[1,8,8,1024]{3,2,1,0:T(8,128)(2,1)S(1)}, bf16[1,8,8,1024]{3,2,1,0:T(8,128)(2,1)S(1)}, u32[]{:S(2)}, u32[]{:S(2)}) collective-permute-start(bf16[1,8,8,1024]{3,2,1,0:T(8,128)(2,1)S(1)} %collective-permute-done.14), channel_id=1, source_target_pairs={{0,15},{1,0},{2,1},{3,2},{4,3},{5,4},{6,5},{7,6},{8,7},{9,8},{10,9... | collective-permute-start | bytes 393224 | tf_op jit(solution)/shard_map/ppermute | solution.py:79
  68.3 7.1 %collective-permute-start.17 = (bf16[1,8,8,1024]{3,2,1,0:T(8,128)(2,1)S(1)}, bf16[1,8,8,1024]{3,2,1,0:T(8,128)(2,1)S(1)}, u32[]{:S(2)}, u32[]{:S(2)}) collective-permute-start(bf16[1,8,8,1024]{3,2,1,0:T(8,128)(2,1)S(1)} %collective-permute-done.15), channel_id=1, source_target_pairs={{0,1},{1,2},{2,3},{3,4},{4,5},{5,6},{6,7},{7,8},{8,9},{9,10},{10,1... | collective-permute-start | bytes 393224 | tf_op jit(solution)/shard_map/ppermute | solution.py:74
  75.4 1.3 copy-start.1
  79.9 3.9 %collective-permute-start = (f32[8,8,1024]{2,1,0:T(8,128)S(1)}, f32[8,8,1024]{2,1,0:T(8,128)S(1)}, u32[]{:S(2)}, u32[]{:S(2)}) collective-permute-start(f32[8,8,1024]{2,1,0:T(8,128)S(1)} %fusion.75), channel_id=1, source_target_pairs={{0,15},{1,0},{2,1},{3,2},{4,3},{5,4},{6,5},{7,6},{8,7},{9,8},{10,9... | collective-permute-start | bytes 786440 | tf_op jit(solution)/shard_map/while/body/eval_jaxpr/ppermute | solution.py:13
  87.1 8.5 %collective-permute-start = (f32[8,8,1024]{2,1,0:T(8,128)S(1)}, f32[8,8,1024]{2,1,0:T(8,128)S(1)}, u32[]{:S(2)}, u32[]{:S(2)}) collective-permute-start(f32[8,8,1024]{2,1,0:T(8,128)S(1)} %fusion.75), channel_id=1, source_target_pairs={{0,15},{1,0},{2,1},{3,2},{4,3},{5,4},{6,5},{7,6},{8,7},{9,8},{10,9... | collective-permute-start | bytes 786440 | tf_op jit(solution)/shard_map/while/body/eval_jaxpr/ppermute | solution.py:13
  98.9 8.5 %collective-permute-start = (f32[8,8,1024]{2,1,0:T(8,128)S(1)}, f32[8,8,1024]{2,1,0:T(8,128)S(1)}, u32[]{:S(2)}, u32[]{:S(2)}) collective-permute-start(f32[8,8,1024]{2,1,0:T(8,128)S(1)} %fusion.75), channel_id=1, source_target_pairs={{0,15},{1,0},{2,1},{3,2},{4,3},{5,4},{6,5},{7,6},{8,7},{9,8},{10,9... | collective-permute-start | bytes 786440 | tf_op jit(solution)/shard_map/while/body/eval_jaxpr/ppermute | solution.py:13
  110.6 8.5 %collective-permute-start = (f32[8,8,1024]{2,1,0:T(8,128)S(1)}, f32[8,8,1024]{2,1,0:T(8,128)S(1)}, u32[]{:S(2)}, u32[]{:S(2)}) collective-permute-start(f32[8,8,1024]{2,1,0:T(8,128)S(1)} %fusion.75), channel_id=1, source_target_pairs={{0,15},{1,0},{2,1},{3,2},{4,3},{5,4},{6,5},{7,6},{8,7},{9,8},{10,9... | collective-permute-start | bytes 786440 | tf_op jit(solution)/shard_map/while/body/eval_jaxpr/ppermute | solution.py:13
  122.4 8.6 %collective-permute-start = (f32[8,8,1024]{2,1,0:T(8,128)S(1)}, f32[8,8,1024]{2,1,0:T(8,128)S(1)}, u32[]{:S(2)}, u32[]{:S(2)}) collective-permute-start(f32[8,8,1024]{2,1,0:T(8,128)S(1)} %fusion.75), channel_id=1, source_target_pairs={{0,15},{1,0},{2,1},{3,2},{4,3},{5,4},{6,5},{7,6},{8,7},{9,8},{10,9... | collective-permute-start | bytes 786440 | tf_op jit(solution)/shard_map/while/body/eval_jaxpr/ppermute | solution.py:13
  134.2 8.5 %collective-permute-start = (f32[8,8,1024]{2,1,0:T(8,128)S(1)}, f32[8,8,1024]{2,1,0:T(8,128)S(1)}, u32[]{:S(2)}, u32[]{:S(2)}) collective-permute-start(f32[8,8,1024]{2,1,0:T(8,128)S(1)} %fusion.75), channel_id=1, source_target_pairs={{0,15},{1,0},{2,1},{3,2},{4,3},{5,4},{6,5},{7,6},{8,7},{9,8},{10,9... | collective-permute-start | bytes 786440 | tf_op jit(solution)/shard_map/while/body/eval_jaxpr/ppermute | solution.py:13
  145.9 8.6 %collective-permute-start = (f32[8,8,1024]{2,1,0:T(8,128)S(1)}, f32[8,8,1024]{2,1,0:T(8,128)S(1)}, u32[]{:S(2)}, u32[]{:S(2)}) collective-permute-start(f32[8,8,1024]{2,1,0:T(8,128)S(1)} %fusion.75), channel_id=1, source_target_pairs={{0,15},{1,0},{2,1},{3,2},{4,3},{5,4},{6,5},{7,6},{8,7},{9,8},{10,9... | collective-permute-start | bytes 786440 | tf_op jit(solution)/shard_map/while/body/eval_jaxpr/ppermute | solution.py:13
  157.7 8.5 %collective-permute-start = (f32[8,8,1024]{2,1,0:T(8,128)S(1)}, f32[8,8,1024]{2,1,0:T(8,128)S(1)}, u32[]{:S(2)}, u32[]{:S(2)}) collective-permute-start(f32[8,8,1024]{2,1,0:T(8,128)S(1)} %fusion.75), channel_id=1, source_target_pairs={{0,15},{1,0},{2,1},{3,2},{4,3},{5,4},{6,5},{7,6},{8,7},{9,8},{10,9... | collective-permute-start | bytes 786440 | tf_op jit(solution)/shard_map/while/body/eval_jaxpr/ppermute | solution.py:13
  169.5 8.6 %collective-permute-start = (f32[8,8,1024]{2,1,0:T(8,128)S(1)}, f32[8,8,1024]{2,1,0:T(8,128)S(1)}, u32[]{:S(2)}, u32[]{:S(2)}) collective-permute-start(f32[8,8,1024]{2,1,0:T(8,128)S(1)} %fusion.75), channel_id=1, source_target_pairs={{0,15},{1,0},{2,1},{3,2},{4,3},{5,4},{6,5},{7,6},{8,7},{9,8},{10,9... | collective-permute-start | bytes 786440 | tf_op jit(solution)/shard_map/while/body/eval_jaxpr/ppermute | solution.py:13
  181.2 8.5 %collective-permute-start = (f32[8,8,1024]{2,1,0:T(8,128)S(1)}, f32[8,8,1024]{2,1,0:T(8,128)S(1)}, u32[]{:S(2)}, u32[]{:S(2)}) collective-permute-start(f32[8,8,1024]{2,1,0:T(8,128)S(1)} %fusion.75), channel_id=1, source_target_pairs={{0,15},{1,0},{2,1},{3,2},{4,3},{5,4},{6,5},{7,6},{8,7},{9,8},{10,9... | collective-permute-start | bytes 786440 | tf_op jit(solution)/shard_map/while/body/eval_jaxpr/ppermute | solution.py:13
  193.0 8.6 %collective-permute-start = (f32[8,8,1024]{2,1,0:T(8,128)S(1)}, f32[8,8,1024]{2,1,0:T(8,128)S(1)}, u32[]{:S(2)}, u32[]{:S(2)}) collective-permute-start(f32[8,8,1024]{2,1,0:T(8,128)S(1)} %fusion.75), channel_id=1, source_target_pairs={{0,15},{1,0},{2,1},{3,2},{4,3},{5,4},{6,5},{7,6},{8,7},{9,8},{10,9... | collective-permute-start | bytes 786440 | tf_op jit(solution)/shard_map/while/body/eval_jaxpr/ppermute | solution.py:13
  204.8 8.5 %collective-permute-start = (f32[8,8,1024]{2,1,0:T(8,128)S(1)}, f32[8,8,1024]{2,1,0:T(8,128)S(1)}, u32[]{:S(2)}, u32[]{:S(2)}) collective-permute-start(f32[8,8,1024]{2,1,0:T(8,128)S(1)} %fusion.75), channel_id=1, source_target_pairs={{0,15},{1,0},{2,1},{3,2},{4,3},{5,4},{6,5},{7,6},{8,7},{9,8},{10,9... | collective-permute-start | bytes 786440 | tf_op jit(solution)/shard_map/while/body/eval_jaxpr/ppermute | solution.py:13
  216.5 8.6 %collective-permute-start = (f32[8,8,1024]{2,1,0:T(8,128)S(1)}, f32[8,8,1024]{2,1,0:T(8,128)S(1)}, u32[]{:S(2)}, u32[]{:S(2)}) collective-permute-start(f32[8,8,1024]{2,1,0:T(8,128)S(1)} %fusion.75), channel_id=1, source_target_pairs={{0,15},{1,0},{2,1},{3,2},{4,3},{5,4},{6,5},{7,6},{8,7},{9,8},{10,9... | collective-permute-start | bytes 786440 | tf_op jit(solution)/shard_map/while/body/eval_jaxpr/ppermute | solution.py:13
  228.3 8.5 %collective-permute-start = (f32[8,8,1024]{2,1,0:T(8,128)S(1)}, f32[8,8,1024]{2,1,0:T(8,128)S(1)}, u32[]{:S(2)}, u32[]{:S(2)}) collective-permute-start(f32[8,8,1024]{2,1,0:T(8,128)S(1)} %fusion.75), channel_id=1, source_target_pairs={{0,15},{1,0},{2,1},{3,2},{4,3},{5,4},{6,5},{7,6},{8,7},{9,8},{10,9... | collective-permute-start | bytes 786440 | tf_op jit(solution)/shard_map/while/body/eval_jaxpr/ppermute | solution.py:13
  240.0 8.6 %collective-permute-start = (f32[8,8,1024]{2,1,0:T(8,128)S(1)}, f32[8,8,1024]{2,1,0:T(8,128)S(1)}, u32[]{:S(2)}, u32[]{:S(2)}) collective-permute-start(f32[8,8,1024]{2,1,0:T(8,128)S(1)} %fusion.75), channel_id=1, source_target_pairs={{0,15},{1,0},{2,1},{3,2},{4,3},{5,4},{6,5},{7,6},{8,7},{9,8},{10,9... | collective-permute-start | bytes 786440 | tf_op jit(solution)/shard_map/while/body/eval_jaxpr/ppermute | solution.py:13
  251.8 8.5 %collective-permute-start = (f32[8,8,1024]{2,1,0:T(8,128)S(1)}, f32[8,8,1024]{2,1,0:T(8,128)S(1)}, u32[]{:S(2)}, u32[]{:S(2)}) collective-permute-start(f32[8,8,1024]{2,1,0:T(8,128)S(1)} %fusion.75), channel_id=1, source_target_pairs={{0,15},{1,0},{2,1},{3,2},{4,3},{5,4},{6,5},{7,6},{8,7},{9,8},{10,9... | collective-permute-start | bytes 786440 | tf_op jit(solution)/shard_map/while/body/eval_jaxpr/ppermute | solution.py:13
